TPU v7x, 32 devices: a whole 2x2x4 slice. The times are simulated.
32 devices in a mesh: tok: 8 (over z, x), head: 4 (over y, core).
Axes of the slice: x: 2, y: 2, z: 4, core: 2. Of those that a mesh axis runs over, the one named last changes fastest.
Arguments:
- queries: bfloat16 [32768, 4, 1024], P('tok', 'head'), as said below
- keys: bfloat16 [32768, 4, 128], P('tok', 'head'), as said below
- basis: float32 [4, 1024, 256], P('head'), may hold values from -0.1875 to 0.1875
Outputs:
- subspace: float32 [4, 1024, 256], P('head')
- keymap: float32 [4, 128, 256], replicated
Inputs may be any that keep to these rules, and one draw needn't show every extreme that they name: `queries`: query features are correlated within a group and share a common part with the keys. `keys`: keys share a common part with the queries of the same tokens.
All inputs are finite; a program needn't handle non-finite values.
Results may differ from a plain program's by a relative error of at most 0.0007.
Values sent between devices are 32-bit elements; how exact they have to be, the bound alone decides.
A program may use at most 64 MiB of HBM per device.

v0:
```python
import jax
import jax.numpy as jnp
from jax import lax
from jax.sharding import PartitionSpec as P

ridge = 0.1
eps = 1e-06
high = lax.Precision.HIGHEST


def orthonormal(image):
    inner = jnp.dot(image.T, image, precision=high)
    lower = jnp.linalg.cholesky(inner)
    return jax.scipy.linalg.solve_triangular(lower, image.T, lower=True).T


def transposed_product(left, right):
    return lax.dot_general(
        left, right, (((0,), (0,)), ((), ())), preferred_element_type=jnp.float32
    )


def on_device(queries, keys, basis):
    query_rows = queries[:, 0, :]
    key_rows = keys[:, 0, :]
    start_basis = basis[0]
    width = query_rows.shape[1]
    total = query_rows.shape[0] * lax.axis_size("tok")
    gram_part = transposed_product(query_rows, query_rows)
    cross_part = transposed_product(key_rows, query_rows)
    gram = lax.psum(gram_part, "tok") / total
    cross_block = lax.psum_scatter(cross_part, "tok", scatter_dimension=0, tiled=True) / total
    scale = jnp.trace(gram) / width + eps
    image = jnp.dot(gram, start_basis, precision=high)
    refined = orthonormal(image)
    small = jnp.dot(refined.T, jnp.dot(gram, refined, precision=high), precision=high)
    rhs = jnp.dot(cross_block, refined, precision=high)
    reduced = small / scale + ridge * jnp.eye(refined.shape[1], dtype=jnp.float32)
    factor = jnp.linalg.cholesky(reduced)
    mapped = jax.scipy.linalg.cho_solve((factor, True), rhs.T).T
    full_map = lax.all_gather(mapped, "tok", axis=0, tiled=True)
    every_map = lax.all_gather(full_map[None], "head", axis=0, tiled=True)
    return (refined[None], every_map)


def solution(mesh):
    placed = (P("tok", "head", None), P("tok", "head", None), P("head", None, None))
    return jax.shard_map(
        on_device,
        mesh=mesh,
        in_specs=placed,
        out_specs=(P("head", None, None), P()),
        check_vma=False,
    )
```

profile of v0, /device:TPU:0, one launch (start us, length us, event | category | flops | bytes accessed | tf_op | source)
XLA Modules:
  0.0 386.5 jit_solution(18145583779490193513)
XLA Ops:
  7.2 0.0 all-reduce.3.cloned.1.call-start
  7.2 15.1 %fusion.2 = f32[1024,1024]{1,0:T(8,128)} fusion(bf16[4096,1,1024]{2,0,1:T(8,128)(2,1)} %param.4), kind=kOutput, calls=%fused_computation.6 | convolution fusion | flops 8589934592 | bytes 12582912 | tf_op jit(solution)/shard_map/dot_general | solution.py:18
  22.4 0.0 reduce-scatter.2.cloned.1.call-start
  22.4 1.1 copy-done.1
  23.6 5.5 %fusion = f32[128,1024]{1,0:T(8,128)} fusion(bf16[4096,1,1024]{2,0,1:T(8,128)(2,1)} %param.4, bf16[4096,1,128]{2,0,1:T(8,128)(2,1)S(1)} %copy-done.1), kind=kOutput, calls=%fused_computation.4 | convolution fusion | flops 1073741824 | bytes 9961472 | tf_op jit(solution)/shard_map/dot_general | solution.py:18
  29.1 152.5 %all-reduce.3.cloned.1.call-done = f32[1024,1024]{1,0:T(8,128)} async-done(((f32[1024,1024]{1,0:T(8,128)}), f32[1024,1024]{1,0:T(8,128)}) %all-reduce.3.cloned.1.call-update) | async-done | bytes 4194320 | tf_op jit(solution)/shard_map/psum | solution.py:31
  181.6 5.5 %fusion.6 = f32[1024,256]{1,0:T(8,128)S(1)} fusion(f32[1024,1024]{1,0:T(8,128)} %all-reduce.3.cloned.1.call-done, f32[1,1024,256]{2,1,0:T(8,128)S(1)} %copy-done), kind=kOutput, calls=%fused_computation.12 | convolution fusion | flops 3222274048 | bytes 6291456 | tf_op jit(solution)/shard_map/dot_general | solution.py:34
  187.1 1.8 fusion.44
  188.9 0.1 copy.5
  189.1 11.7 %cholesky.130 = f32[128,128]{1,0:T(8,128)S(1)} custom-call(f32[128,128]{1,0:T(8,128)S(1)} %cholesky.194), custom_call_target="Cholesky" | custom-call | tf_op jit(solution)/shard_map/jit(cholesky)/cholesky | solution.py:13
  200.9 9.8 %custom-call.22 = f32[1,128,128]{1,2,0:T(8,128)S(1)} custom-call(f32[1,128,128]{2,1,0:T(8,128)S(1)} %get-tuple-element.52), custom_call_target="InvertDiagBlocksLowerTriangular" | custom-call | tf_op jit(solution)/shard_map/jit(cholesky)/cholesky | solution.py:13
  210.7 0.2 fusion.23
  210.9 0.3 convolution_subtract_fusion.2
  211.2 11.7 %cholesky.147 = f32[128,128]{1,0:T(8,128)S(1)} custom-call(f32[128,128]{1,0:T(8,128)S(1)} %convolution_subtract_fusion.2), custom_call_target="Cholesky" | custom-call | tf_op jit(solution)/shard_map/jit(cholesky)/cholesky | solution.py:13
  222.9 0.1 copy.8
  223.0 0.1 copy.7
  223.1 0.1 copy.6
  223.2 13.7 %compare_reduce_fusion.2 = (pred[]{:T(512)}, pred[]{:T(512)}) fusion(f32[128]{0:T(128)S(1)} %select_reduce_fusion.3, f32[128]{0:T(128)S(1)} %get-tuple-element.51), kind=kLoop, calls=%fused_computation.70 | loop fusion | flops 510 | bytes 1026 | tf_op jit(solution)/shard_map/jit(cholesky)/cholesky | solution.py:13
  238.2 0.1 triangular_solve.107
  238.3 4.1 %while.2 = (s32[]{:T(128)}, f32[256,256]{0,1:T(8,128)S(1)}, s32[2,2]{1,0:T(2,128)S(1)}, f32[2,128,128]{2,1,0:T(8,128)S(1)}, s32[]{:T(128)}) while((s32[]{:T(128)}, f32[256,256]{0,1:T(8,128)S(1)}, s32[2,2]{1,0:T(2,128)S(1)}, f32[2,128,128]{2,1,0:T(8,128)S(1)}, s32[]{:T(128)}) %tuple.44), condition=%wide.while_cond, body=%wide.while_body.sunk | while | flops 2 | bytes 393321 | solution.py:14
  238.4 0.6 fusion.61
  239.0 1.3 dynamic-slice.13
  240.3 0.1 copy.22
  240.4 0.6 fusion.61
  241.0 1.3 dynamic-slice.13
  242.3 0.1 copy.22
  242.4 19.7 %custom-call.19 = f32[2,128,128]{1,2,0:T(8,128)S(1)} custom-call(f32[2,128,128]{2,1,0:T(8,128)S(1)} %get-tuple-element.10), custom_call_target="InvertDiagBlocksLowerTriangular" | custom-call | tf_op jit(solution)/shard_map/jit(_solve_triangular)/triangular_solve | solution.py:14
  262.1 0.6 fusion.13
  262.8 1.0 convolution_subtract_fusion
  263.8 0.6 fusion.22
  264.4 2.9 select_reduce_fusion
  268.0 5.3 %fusion.4 = f32[1024,256]{1,0:T(8,128)S(1)} fusion(f32[1024,1024]{1,0:T(8,128)} %all-reduce.3.cloned.1.call-done, f32[128,1024]{1,0:T(8,128)S(1)} %fusion.22, f32[128,1024]{1,0:T(8,128)S(1)} %fusion.13), kind=kOutput, calls=%fused_computation.10 | convolution fusion | flops 3222536192 | bytes 6291456 | tf_op jit(solution)/shard_map/dot_general | solution.py:36
  273.3 1.9 fusion.10
  275.2 0.1 copy.11
  275.4 11.7 %cholesky.164 = f32[128,128]{1,0:T(8,128)S(1)} custom-call(f32[128,128]{1,0:T(8,128)S(1)} %cholesky.197), custom_call_target="Cholesky" | custom-call | tf_op jit(solution)/shard_map/jit(cholesky)/cholesky | solution.py:39
  287.1 9.8 %custom-call.23 = f32[1,128,128]{1,2,0:T(8,128)S(1)} custom-call(f32[1,128,128]{2,1,0:T(8,128)S(1)} %get-tuple-element.50), custom_call_target="InvertDiagBlocksLowerTriangular" | custom-call | tf_op jit(solution)/shard_map/jit(cholesky)/cholesky | solution.py:39
  296.9 0.2 fusion.19
  297.2 0.3 convolution_subtract_fusion.1
  297.4 11.7 %cholesky.181 = f32[128,128]{1,0:T(8,128)S(1)} custom-call(f32[128,128]{1,0:T(8,128)S(1)} %convolution_subtract_fusion.1), custom_call_target="Cholesky" | custom-call | tf_op jit(solution)/shard_map/jit(cholesky)/cholesky | solution.py:39
  309.2 0.1 copy.14
  309.3 0.1 copy.13
  309.4 0.1 copy.12
  309.5 0.8 compare_reduce_fusion
  310.3 0.7 compare_reduce_fusion.1
  312.4 4.3 %while.3 = (s32[]{:T(128)}, f32[256,256]{0,1:T(8,128)S(1)}, s32[2,2]{1,0:T(2,128)S(1)}, f32[2,128,128]{2,1,0:T(8,128)S(1)}, s32[]{:T(128)}) while((s32[]{:T(128)}, f32[256,256]{0,1:T(8,128)S(1)}, s32[2,2]{1,0:T(2,128)S(1)}, f32[2,128,128]{2,1,0:T(8,128)S(1)}, s32[]{:T(128)}) %tuple.56), condition=%wide.while_cond.1, body=%wide.while_body.1.sunk | while | flops 2 | bytes 393321 | solution.py:40
  312.4 0.7 fusion.62
  313.1 1.3 dynamic-slice.15
  314.4 0.1 copy.23
  314.6 0.7 fusion.62
  315.2 1.3 dynamic-slice.15
  316.6 0.1 copy.23
  316.7 19.7 %custom-call.20 = f32[2,128,128]{1,2,0:T(8,128)S(1)} custom-call(f32[2,128,128]{2,1,0:T(8,128)S(1)} %get-tuple-element.18), custom_call_target="InvertDiagBlocksLowerTriangular" | custom-call | tf_op jit(solution)/shard_map/jit(_cho_solve)/triangular_solve | solution.py:40
  336.4 0.1 fusion.16
  336.5 1.8 fusion.15
  338.3 0.2 fusion.29
  338.4 0.2 convolution_subtract_fusion.4
  338.6 0.3 fusion.31
  338.9 0.2 fusion.30
  339.2 0.2 convolution_subtract_fusion.3
  339.4 0.2 fusion.28
  339.6 30.6 %all_gather.6 = f32[128,256]{1,0:T(8,128)S(1)} all-gather(f32[16,256]{1,0:T(8,128)S(1)} %maximum_bitcast_fusion), channel_id=1, replica_groups=mesh['tok'=8,'head'=4] {'tok'}, dimensions={0}, use_global_device_ids=true | all-gather | bytes 147456 | tf_op jit(solution)/shard_map/all_gather | solution.py:41
  370.2 7.1 %all-gather = f32[512,256]{1,0:T(8,128)S(1)} all-gather(f32[128,256]{1,0:T(8,128)S(1)} %all_gather.6), channel_id=2, replica_groups=mesh['tok'=8,'head'=4] {'head'}, dimensions={0}, use_global_device_ids=true | all-gather | bytes 655360 | tf_op jit(solution)/shard_map/all_gather | solution.py:42
  377.3 1.3 copy.16
  378.6 0.8 copy.48
  (34 shorter events, 0.5 us)
Async XLA Ops:
  7.2 174.4 %copy-start = (f32[1,1024,256]{2,1,0:T(8,128)S(1)}, f32[1,1024,256]{2,1,0:T(8,128)}, u32[]{:S(2)}) copy-start(f32[1,1024,256]{2,1,0:T(8,128)} %param.6) | copy-start | bytes 3145732
  7.2 174.4 %all-reduce.3.cloned.1.call-start = ((), (), s32[]{:S(2)}) async-start(), calls=%async_computation.1 | async-start | bytes 8388608 | tf_op jit(solution)/shard_map/psum | solution.py:31
  22.4 1.2 copy-start.1
  22.4 314.1 %reduce-scatter.2.cloned.1.call-start = ((), (), s32[]{:S(2)}) async-start(), calls=%async_computation.2 | async-start | bytes 589824 | tf_op jit(solution)/shard_map/reduce_scatter | solution.py:32
Sparse Core Ops, SparseCore 0:
  22.5 159.0 all-reduce.2
  185.5 61.1 reduce-scatter.1
where the time goes:
time: 386 us
  waiting for transfers between devices  153 us (40%)
  other arithmetic  124 us (32%)
  matrix products  41.4 us (11%)
  blocking collectives  37.7 us (10%)
  between operations  17.7 us (5%)
  local copies, waits for them, and re-layouts  12.5 us (3%)
    psum x1, waiting for transfers between devices, on_device(): gram = lax.psum(gram_part, 'tok') / total  152 us
    another operation x6, other arithmetic, orthonormal(): lower = jnp.linalg.cholesky(inner)  47 us
    another operation x7, other arithmetic, on_device(): factor = jnp.linalg.cholesky(reduced)  34.9 us
    all_gather x1, blocking collectives, on_device(): full_map = lax.all_gather(mapped, 'tok', axis=0, tiled=True)  30.6 us
    dot_general x2, matrix products, transposed_product(): lax.dot_general(left, right, (((0,), (0,)), ((), ())), preferred_element_...  20.6 us
    another operation x3, other arithmetic, orthonormal(): return jax.scipy.linalg.solve_triangular(lower, image.T, lower=True).T  19.7 us
    another operation x2, other arithmetic, on_device(): mapped = jax.scipy.linalg.cho_solve((factor, True), rhs.T).T  19.7 us
    another operation x20, local copies, waits for them, and re-layouts  8.25 us
  transfers between devices with their start and end apart: 2, of which 1 were waited for; matrix products, arithmetic and copies ran while one was open for 41% of the time, Pallas kernels for 0%

commit v1 on v0

--- a/solution.py
+++ b/solution.py
@@ -25,21 +25,22 @@
     key_rows = keys[:, 0, :]
     start_basis = basis[0]
     width = query_rows.shape[1]
+    rank = start_basis.shape[1]
     total = query_rows.shape[0] * lax.axis_size("tok")
-    gram_part = transposed_product(query_rows, query_rows)
-    cross_part = transposed_product(key_rows, query_rows)
-    gram = lax.psum(gram_part, "tok") / total
-    cross_block = lax.psum_scatter(cross_part, "tok", scatter_dimension=0, tiled=True) / total
-    scale = jnp.trace(gram) / width + eps
-    image = jnp.dot(gram, start_basis, precision=high)
+    gram_part = transposed_product(query_rows, query_rows) / total
+    cross_part = transposed_product(key_rows, query_rows) / total
+    image = lax.psum(jnp.dot(gram_part, start_basis, precision=high), "tok")
     refined = orthonormal(image)
-    small = jnp.dot(refined.T, jnp.dot(gram, refined, precision=high), precision=high)
-    rhs = jnp.dot(cross_block, refined, precision=high)
-    reduced = small / scale + ridge * jnp.eye(refined.shape[1], dtype=jnp.float32)
+    small_part = jnp.dot(refined.T, jnp.dot(gram_part, refined, precision=high), precision=high)
+    rhs_part = jnp.dot(cross_part, refined, precision=high)
+    trace_part = jnp.full((8, rank), jnp.trace(gram_part))
+    packed = lax.psum(jnp.concatenate([small_part, rhs_part, trace_part], axis=0), "tok")
+    small, rhs, trace = packed[:rank], packed[rank:-8], packed[-1, 0]
+    scale = trace / width + eps
+    reduced = small / scale + ridge * jnp.eye(rank, dtype=jnp.float32)
     factor = jnp.linalg.cholesky(reduced)
     mapped = jax.scipy.linalg.cho_solve((factor, True), rhs.T).T
-    full_map = lax.all_gather(mapped, "tok", axis=0, tiled=True)
-    every_map = lax.all_gather(full_map[None], "head", axis=0, tiled=True)
+    every_map = lax.all_gather(mapped[None], "head", axis=0, tiled=True)
     return (refined[None], every_map)
 
 

time: 386 us -> 346 us (0.90); the launches traced: 386 us -> 340 us
  blocking collectives: 37.7 us -> 7.15 us
  other arithmetic: 124 us -> 112 us
  waiting for transfers between devices: 153 us -> 146 us
  local copies, waits for them, and re-layouts: 12.5 us -> 16.5 us
    all_gather x2 -> x1, blocking collectives: 37.7 us -> 7.15 us  [on_device(): every_map = lax.all_gather(mapped[None], 'head', axis=0, tiled=True)]
    another operation x6, other arithmetic: 47 us -> 34.5 us  [orthonormal(): lower = jnp.linalg.cholesky(inner)]
    psum x1 -> x2, waiting for transfers between devices: 152 us -> 146 us  [the longest x1 75.2 us: on_device(): image = lax.psum(jnp.dot(gram_part, start_basis, precision=high), 'tok')]
  transfers between devices with their start and end apart: 2 -> 2, of which waited for: 1 -> 2; matrix products, arithmetic and copies ran while one was open for 41% -> 2% of each run, Pallas kernels for 0% -> 0%
where the time goes in v1:
time: 346 us; the launch traced here: 340 us
  waiting for transfers between devices  146 us (42%)
  other arithmetic  112 us (32%)
  matrix products  40.5 us (12%)
  between operations  18 us (5%)
  local copies, waits for them, and re-layouts  16.5 us (5%)
  blocking collectives  7.15 us (2%)
    psum x1, waiting for transfers between devices, on_device(): image = lax.psum(jnp.dot(gram_part, start_basis, precision=high), 'tok')  75.2 us
    psum x1, waiting for transfers between devices, on_device(): lax.psum(jnp.concatenate([small_part, rhs_part, trace_part], axis=0), 'tok')  70.7 us
    another operation x7, other arithmetic, on_device(): factor = jnp.linalg.cholesky(reduced)  34.8 us
    another operation x6, other arithmetic, orthonormal(): lower = jnp.linalg.cholesky(inner)  34.5 us
    another operation x3, other arithmetic, orthonormal(): return jax.scipy.linalg.solve_triangular(lower, image.T, lower=True).T  19.7 us
    another operation x2, other arithmetic, on_device(): mapped = jax.scipy.linalg.cho_solve((factor, True), rhs.T).T  19.7 us
    dot_general x2, matrix products, transposed_product(): lax.dot_general(left, right, (((0,), (0,)), ((), ())), preferred_element_...  19.6 us
    another operation x20, local copies, waits for them, and re-layouts  8.41 us
  transfers between devices with their start and end apart: 2, of which 2 were waited for; matrix products, arithmetic and copies ran while one was open for 2% of the time, Pallas kernels for 0%

profile of v1, /device:TPU:0, one launch (start us, length us, event | category | flops | bytes accessed | tf_op | source)
XLA Modules:
  0.0 340.3 jit_solution(13196558192718863227)
XLA Ops:
  7.2 15.0 %select_reduce_fusion = (f32[]{:T(128)}, f32[1024,1024]{1,0:T(8,128)S(1)}) fusion(bf16[4096,1,1024]{2,0,1:T(8,128)(2,1)} %param.4), kind=kOutput, calls=%fused_computation.8 | convolution fusion | flops 8594128896 | bytes 12582916 | tf_op jit(solution)/shard_map/dot_general | solution.py:18
  22.2 1.9 copy-done.1
  24.1 4.4 %fusion.6 = f32[1024,256]{1,0:T(8,128)} fusion(f32[1024,1024]{1,0:T(8,128)S(1)} %get-tuple-element.54, f32[1,1024,256]{2,1,0:T(8,128)S(1)} %copy-done), kind=kOutput, calls=%fused_computation.12 | convolution fusion | flops 3222274048 | bytes 6291456 | tf_op jit(solution)/shard_map/dot_general | solution.py:32
  28.6 0.3 all-reduce.6.cloned.1.call-start
  28.9 0.6 broadcast_in_dim.16
  29.6 4.7 %fusion.10 = f32[128,1024]{1,0:T(8,128)S(1)} fusion(bf16[4096,1,1024]{2,0,1:T(8,128)(2,1)} %param.4, bf16[4096,1,128]{2,0,1:T(8,128)(2,1)S(1)} %copy-done.3), kind=kOutput, calls=%fused_computation.17 | convolution fusion | flops 1073872896 | bytes 9961472 | tf_op jit(solution)/shard_map/dot_general | solution.py:18
  34.3 75.2 %all-reduce.4.cloned.1.call-done = f32[1024,256]{1,0:T(8,128)} async-done(((f32[1024,256]{1,0:T(8,128)}), f32[1024,256]{1,0:T(8,128)}) %all-reduce.4.cloned.1.call-update) | async-done | bytes 1048592 | tf_op jit(solution)/shard_map/psum | solution.py:32
  109.4 3.4 %fusion.45 = f32[256,256]{1,0:T(8,128)S(1)} fusion(f32[1024,256]{1,0:T(8,128)} %all-reduce.4.cloned.1.call-done), kind=kOutput, calls=%fused_computation.86 | convolution fusion | flops 805306368 | bytes 1310720 | tf_op jit(solution)/shard_map/dot_general | solution.py:12
  112.9 0.1 copy.5
  113.1 11.7 %cholesky.130 = f32[128,128]{1,0:T(8,128)S(1)} custom-call(f32[128,128]{1,0:T(8,128)S(1)} %cholesky.194), custom_call_target="Cholesky" | custom-call | tf_op jit(solution)/shard_map/jit(cholesky)/cholesky | solution.py:13
  124.8 9.8 %custom-call.22 = f32[1,128,128]{1,2,0:T(8,128)S(1)} custom-call(f32[1,128,128]{2,1,0:T(8,128)S(1)} %get-tuple-element.52), custom_call_target="InvertDiagBlocksLowerTriangular" | custom-call | tf_op jit(solution)/shard_map/jit(cholesky)/cholesky | solution.py:13
  134.7 0.2 fusion.29
  134.9 0.3 convolution_subtract_fusion.4
  135.1 12.2 %cholesky.147 = f32[128,128]{1,0:T(8,128)S(1)} custom-call(f32[128,128]{1,0:T(8,128)S(1)} %convolution_subtract_fusion.4), custom_call_target="Cholesky" | custom-call | tf_op jit(solution)/shard_map/jit(cholesky)/cholesky | solution.py:13
  147.4 0.1 copy.8
  147.5 0.1 copy.7
  147.6 0.1 copy.6
  147.7 0.6 compare_reduce_fusion.2
  149.8 4.2 %while.2 = (s32[]{:T(128)}, f32[256,256]{0,1:T(8,128)S(1)}, s32[2,2]{1,0:T(2,128)S(1)}, f32[2,128,128]{2,1,0:T(8,128)S(1)}, s32[]{:T(128)}) while((s32[]{:T(128)}, f32[256,256]{0,1:T(8,128)S(1)}, s32[2,2]{1,0:T(2,128)S(1)}, f32[2,128,128]{2,1,0:T(8,128)S(1)}, s32[]{:T(128)}) %tuple.45), condition=%wide.while_cond, body=%wide.while_body.sunk | while | flops 2 | bytes 393321 | solution.py:14
  149.9 0.6 fusion.63
  150.4 1.4 dynamic-slice.13
  151.8 0.1 copy.26
  152.0 0.6 fusion.63
  152.6 1.4 dynamic-slice.13
  154.1 19.7 %custom-call.19 = f32[2,128,128]{1,2,0:T(8,128)S(1)} custom-call(f32[2,128,128]{2,1,0:T(8,128)S(1)} %get-tuple-element.10), custom_call_target="InvertDiagBlocksLowerTriangular" | custom-call | tf_op jit(solution)/shard_map/jit(_solve_triangular)/triangular_solve | solution.py:14
  173.8 0.6 fusion.15
  174.4 1.0 convolution_subtract_fusion
  175.4 0.6 fusion.28
  176.1 5.5 %fusion.4 = f32[1024,256]{1,0:T(8,128)S(1)} fusion(f32[1024,1024]{1,0:T(8,128)} %copy-done.1, f32[128,1024]{1,0:T(8,128)S(1)} %fusion.28, f32[128,1024]{1,0:T(8,128)S(1)} %fusion.15), kind=kOutput, calls=%fused_computation.10 | convolution fusion | flops 3222536192 | bytes 6291456 | tf_op jit(solution)/shard_map/dot_general | solution.py:34
  181.5 1.9 fusion.18
  183.4 1.0 fusion.17
  184.4 0.9 maximum_maximum_fusion
  185.3 0.1 fusion.19
  185.4 1.3 copy.17
  186.7 70.7 %all-reduce.6.cloned.1.call-done = f32[392,256]{0,1:T(8,128)} async-done(((f32[392,256]{0,1:T(8,128)}), f32[392,256]{0,1:T(8,128)}) %all-reduce.6.cloned.1.call-update) | async-done | bytes 401424 | tf_op jit(solution)/shard_map/psum | solution.py:37
  257.4 1.3 slice.103
  259.3 1.0 fusion.20
  260.3 0.1 copy.12
  260.5 1.0 fusion.21
  261.5 11.7 %cholesky.164 = f32[128,128]{1,0:T(8,128)S(1)} custom-call(f32[128,128]{1,0:T(8,128)S(1)} %cholesky.197), custom_call_target="Cholesky" | custom-call | tf_op jit(solution)/shard_map/jit(cholesky)/cholesky | solution.py:41
  273.2 9.8 %custom-call.23 = f32[1,128,128]{1,2,0:T(8,128)S(1)} custom-call(f32[1,128,128]{2,1,0:T(8,128)S(1)} %get-tuple-element.50), custom_call_target="InvertDiagBlocksLowerTriangular" | custom-call | tf_op jit(solution)/shard_map/jit(cholesky)/cholesky | solution.py:41
  283.1 0.2 fusion.25
  283.3 0.3 convolution_subtract_fusion.3
  283.5 11.9 %cholesky.181 = f32[128,128]{1,0:T(8,128)S(1)} custom-call(f32[128,128]{1,0:T(8,128)S(1)} %convolution_subtract_fusion.3), custom_call_target="Cholesky" | custom-call | tf_op jit(solution)/shard_map/jit(cholesky)/cholesky | solution.py:41
  295.5 0.1 copy.15
  295.6 0.1 copy.14
  295.7 0.1 copy.13
  295.8 0.7 compare_reduce_fusion
  296.5 0.6 compare_reduce_fusion.1
  298.6 4.3 %while.3 = (s32[]{:T(128)}, f32[256,256]{0,1:T(8,128)S(1)}, s32[2,2]{1,0:T(2,128)S(1)}, f32[2,128,128]{2,1,0:T(8,128)S(1)}, s32[]{:T(128)}) while((s32[]{:T(128)}, f32[256,256]{0,1:T(8,128)S(1)}, s32[2,2]{1,0:T(2,128)S(1)}, f32[2,128,128]{2,1,0:T(8,128)S(1)}, s32[]{:T(128)}) %tuple.55), condition=%wide.while_cond.1, body=%wide.while_body.1.sunk | while | flops 2 | bytes 393321 | solution.py:42
  298.6 0.6 fusion.64
  299.2 1.4 dynamic-slice.15
  300.8 0.6 fusion.64
  301.4 1.4 dynamic-slice.15
  302.9 19.7 %custom-call.20 = f32[2,128,128]{1,2,0:T(8,128)S(1)} custom-call(f32[2,128,128]{2,1,0:T(8,128)S(1)} %get-tuple-element.18), custom_call_target="InvertDiagBlocksLowerTriangular" | custom-call | tf_op jit(solution)/shard_map/jit(_cho_solve)/triangular_solve | solution.py:42
  322.6 0.9 slice_bitcast_fusion
  323.5 0.3 fusion.23
  323.8 0.3 convolution_subtract_fusion.2
  324.1 0.3 fusion.35
  324.4 0.2 fusion.34
  324.6 0.2 convolution_subtract_fusion.1
  324.8 0.2 fusion.33
  325.1 7.2 %all-gather = f32[512,256]{0,1:T(8,128)S(1)} all-gather(f32[128,256]{0,1:T(8,128)S(1)} %maximum_bitcast_fusion), channel_id=2, replica_groups=mesh['tok'=8,'head'=4] {'head'}, dimensions={0}, use_global_device_ids=true | all-gather | bytes 655360 | tf_op jit(solution)/shard_map/all_gather | solution.py:43
  332.2 1.0 copy.21
  (42 shorter events, 0.9 us)
Async XLA Ops:
  7.2 17.0 %copy-start = (f32[1,1024,256]{2,1,0:T(8,128)S(1)}, f32[1,1024,256]{2,1,0:T(8,128)}, u32[]{:S(2)}) copy-start(f32[1,1024,256]{2,1,0:T(8,128)} %param.6) | copy-start | bytes 3145732
  7.2 102.3 %all-reduce.4.cloned.1.call-start = ((), (), s32[]{:S(2)}) async-start(), calls=%async_computation | async-start | bytes 2097152 | tf_op jit(solution)/shard_map/psum | solution.py:32
  22.2 1.9 copy-start.1
  22.2 7.4 %copy-start.3 = (bf16[4096,1,128]{2,0,1:T(8,128)(2,1)S(1)}, bf16[4096,1,128]{2,0,1:T(8,128)(2,1)}, u32[]{:S(2)}) copy-start(bf16[4096,1,128]{2,0,1:T(8,128)(2,1)} %param.5) | copy-start | bytes 3145732
  28.6 228.9 %all-reduce.6.cloned.1.call-start = ((), (), s32[]{:S(2)}) async-start(), calls=%async_computation.1 | async-start | bytes 1048576 | tf_op jit(solution)/shard_map/psum | solution.py:37
  109.4 64.3 %copy-start.2 = (f32[1024,256]{1,0:T(8,128)S(1)}, f32[1024,256]{1,0:T(8,128)}, u32[]{:S(2)}) copy-start(f32[1024,256]{1,0:T(8,128)} %all-reduce.4.cloned.1.call-done) | copy-start | bytes 3145732
Sparse Core Ops, SparseCore 0:
  28.7 80.7 all-reduce.3
  185.4 71.9 all-reduce.5
